TPU v7x, 32 devices: a whole 2x2x4 slice. The times are simulated.
32 devices in a mesh: leaf: 16 (over z, y, x), cone: 2 (over core).
Axes of the slice: x: 2, y: 2, z: 4, core: 2. Of those that a mesh axis runs over, the one named last changes fastest.
Arguments:
- coefficients: bfloat16 [128, 4, 3, 32, 256], P('leaf', 'cone'), may hold values from -6 to 6
- local_to_target: bfloat16 [128, 4, 256, 768], P('leaf', 'cone'), may hold values from -0.1875 to 0.1875
- send_map: int32 [16, 16, 32], P('leaf'), may hold values from -1 to 255, as said below
- test_weight: bfloat16 [16, 16, 32, 108], P('leaf'), may hold values from -1 to 1
- slot_edge: int32 [3, 16, 16, 32], P(None, 'leaf'), may hold values from -1 to 383, as said below
- shared_edges: int32 [16, 2, 32], P('leaf'), may hold values from 0 to 383, as said below
Outputs:
- tested: float32 [2, 32, 6144], P(None, 'cone', 'leaf')
Inputs may be any that keep to these rules, and one draw needn't show every extreme that they name: Each of the 256 triangles of a leaf device s stands in exactly one slot of send_map[s]; every other slot is -1. In every draw, each leaf device fills all 32 slots of its block to some owner. slot_edge[e, d, s, n] is -1 exactly where send_map[s, d, n] is -1. The 64 numbers of shared_edges[d] are distinct.
All inputs are finite; a program needn't handle non-finite values.
Results may differ from a plain program's by a relative error of at most 0.0029.
Values may be sent and summed in bfloat16 or wider, within the bound.
A program may use at most 64 MiB of HBM per device.

v0:
```python
import jax
import jax.numpy as jnp
from jax import lax
from jax.sharding import PartitionSpec as P

QUAD = 12
TRI_LEAF = 32
EDGE_DEV = 384


def extended(array, sides, width):
    for axis, dim in sides:
        peers, length = (lax.axis_size(axis), array.shape[dim])
        up = [(i, (i + 1) % peers) for i in range(peers - 1)]
        down = [(j, i) for i, j in up]
        last = lax.slice_in_dim(array, length - width, length, axis=dim)
        leading = lax.slice_in_dim(array, 0, width, axis=dim)
        before = lax.ppermute(last, axis, up)
        after = lax.ppermute(leading, axis, down)
        array = jnp.concatenate([before, array, after], axis=dim)
    return array


def tested_slots(weights, fields, rhs_count, result_form):
    peer_count, capacity = (weights.shape[0], weights.shape[1])
    weight_view = weights.reshape(peer_count, capacity, 3, QUAD, 3)
    field_view = fields.reshape(peer_count, capacity, QUAD, 2, 3, rhs_count)
    return jnp.einsum(
        "scepk,scpikh->" + result_form, weight_view, field_view, preferred_element_type=jnp.float32
    )


def body(coefficients, local_to_target, send_map, test_weight, slot_edge, shared_edges):
    partial_field = jnp.einsum(
        "lkchr,lkrq->lqch", coefficients, local_to_target, preferred_element_type=jnp.float32
    )
    cone_count = lax.axis_size("cone")
    rhs_count = partial_field.shape[3] // cone_count
    summed = lax.psum(partial_field, "cone")
    rhs_share = lax.dynamic_slice_in_dim(summed, lax.axis_index("cone") * rhs_count, rhs_count, 3)
    rhs_share = rhs_share.astype(jnp.bfloat16)
    leaf_count = rhs_share.shape[0]
    tri_rows = rhs_share.reshape(leaf_count * TRI_LEAF, -1)
    send_rows = send_map[0]
    is_live = send_rows >= 0
    safe_rows = jnp.where(is_live, send_rows, 0)
    picked = tri_rows[safe_rows]
    outgoing = jnp.where(is_live[:, :, None], picked, jnp.zeros((), jnp.bfloat16))
    weights = test_weight[0]
    arrived = lax.all_to_all(outgoing, "leaf", split_axis=0, concat_axis=0, tiled=True)
    partial_value = tested_slots(weights, arrived, rhs_count, "escih")
    edge_ids = slot_edge[:, 0].reshape(-1)
    values = partial_value.reshape(-1, 2 * rhs_count)
    onehot = (edge_ids[:, None] == jnp.arange(EDGE_DEV, dtype=jnp.int32)[None, :]).astype(
        jnp.float32
    )
    edge_sum = jnp.einsum(
        "ra,re->ae",
        values,
        onehot,
        precision=lax.Precision.HIGHEST,
        preferred_element_type=jnp.float32,
    )
    lower_ids = shared_edges[0, 0]
    upper_ids = shared_edges[0, 1]
    share_width = lower_ids.shape[0]
    rim_values = jnp.concatenate([edge_sum[:, lower_ids], edge_sum[:, upper_ids]], axis=1)
    padded = extended(rim_values, (("leaf", 1),), share_width)
    total = (
        edge_sum.at[:, lower_ids]
        .add(padded[:, :share_width])
        .at[:, upper_ids]
        .add(padded[:, 3 * share_width :])
    )
    return total.reshape(2, rhs_count, -1)


def solution(mesh):
    placed = (
        P("leaf", "cone", None, None, None),
        P("leaf", "cone", None, None),
        P("leaf", None, None),
        P("leaf", None, None, None),
        P(None, "leaf", None, None),
        P("leaf", None, None),
    )
    return jax.shard_map(
        body, mesh=mesh, in_specs=placed, out_specs=P(None, "cone", "leaf"), check_vma=False
    )
```

profile of v0, /device:TPU:6, one launch (start us, length us, event | category | flops | bytes accessed | tf_op | source)
XLA Modules:
  0.0 120.5 jit_solution(16568541062340450514)
XLA Ops:
  0.0 0.0 copy-start
  0.0 0.8 compare_select_fusion
  0.8 0.7 compare_bitcast_fusion
  1.5 0.0 copy-done
  1.5 5.3 %fusion.3 = f32[8,768,3,32]{1,3,2,0:T(8,128)} fusion(bf16[8,2,3,32,256]{4,3,2,1,0:T(8,128)(2,1)S(1)} %copy-done, bf16[8,2,256,768]{3,2,1,0:T(8,128)(2,1)} %param.7), kind=kOutput, calls=%fused_computation.9 | convolution fusion | flops 603979776 | bytes 9437184 | tf_op jit(solution)/shard_map/lkchr,lkrq->lqch/dot_general | solution.py:34
  6.8 10.3 %all-reduce.1 = bf16[8,768,3,32]{1,3,2,0:T(8,128)(2,1)S(1)} all-reduce(f32[8,768,3,32]{1,3,2,0:T(8,128)} %fusion.3), channel_id=1, replica_groups=mesh['leaf'=16,'cone'=2] {'cone'}, use_global_device_ids=true, to_apply=%region_0.0 | all-reduce | flops 589824 | bytes 3538944 | tf_op jit(solution)/shard_map/psum | solution.py:39
  17.1 6.7 %copy.25 = bf16[8,768,3,16]{3,2,1,0:T(4,128)(2,1)} copy(bf16[8,768,3,16]{1,3,2,0:T(8,128)(2,1)S(1)} %dynamic-slice_convert_fusion) | data formatting | bytes 1179648 | tf_op jit(solution)/shard_map/convert_element_type | solution.py:41
  23.9 9.3 %reshape.102 = bf16[256,1152]{1,0:T(8,128)(2,1)S(1)} reshape(bf16[8,768,3,16]{3,2,1,0:T(4,128)(2,1)} %copy.25) | data formatting | bytes 1179648 | tf_op jit(solution)/shard_map/reshape | solution.py:43
  33.2 0.1 reshape.108
  33.3 2.1 %gather_fusion = bf16[512,1152]{1,0:T(8,128)(2,1)S(1)} fusion(bf16[256,1152]{1,0:T(8,128)(2,1)S(1)} %reshape.102, s32[1024]{0:T(1024)S(1)} %pad_clamp_fusion.2), kind=kCustom, calls=%fused_computation | custom fusion | bytes 2361344 | tf_op jit(solution)/shard_map/gather | solution.py:47
  35.4 0.0 copy-start.2
  35.4 1.2 %broadcast_select_fusion = bf16[16,32,1152]{2,1,0:T(8,128)(2,1)} fusion(bf16[16,32,1152]{2,1,0:T(8,128)(2,1)S(1)} %bitcast.58, pred[16,32]{1,0:T(8,128)(4,1)S(1)} %compare_bitcast_fusion), kind=kLoop, calls=%fused_computation.13 | loop fusion | flops 589824 | bytes 2359808 | tf_op jit(solution)/shard_map/jit(_where)/select_n | solution.py:48
  36.6 0.0 copy-start.3
  36.6 0.0 copy-start.4
  36.6 7.4 %all-to-all-start = ((bf16[16,32,1152]{2,1,0:T(8,128)(2,1)}), bf16[16,32,1152]{2,1,0:T(8,128)(2,1)S(1)}, u32[]{:S(2)}, u32[]{:S(2)}) async-start(bf16[16,32,1152]{2,1,0:T(8,128)(2,1)} %broadcast_select_fusion), calls=%async_computation | async-start | bytes 2359296 | tf_op jit(solution)/shard_map/all_to_all | solution.py:50
  44.0 0.0 copy-done.2
  44.0 0.4 copy.27
  44.4 2.5 %copy.37 = bf16[16,32,3,12,3,1]{3,2,4,5,1,0:T(4,128)(2,1)} copy(bf16[16,32,3,12,3,1]{1,0,4,3,2,5:T(8,128)(2,1)S(1)} %bitcast.59) | data formatting | bytes 221184 | tf_op jit(solution)/shard_map/reshape;squeeze | solution.py:26
  47.0 0.0 copy-done.3
  47.0 0.1 eq.15
  47.1 0.0 copy-done.4
  47.1 23.8 %all-to-all-done = bf16[16,32,1152]{2,1,0:T(8,128)(2,1)S(1)} async-done(((bf16[16,32,1152]{2,1,0:T(8,128)(2,1)}), bf16[16,32,1152]{2,1,0:T(8,128)(2,1)S(1)}, u32[]{:S(2)}, u32[]{:S(2)}) %all-to-all-start) | async-done | bytes 1179680 | tf_op jit(solution)/shard_map/all_to_all | solution.py:50
  70.9 3.3 %copy.26 = bf16[16,32,1152]{1,2,0:T(8,128)(2,1)} copy(bf16[16,32,1152]{2,1,0:T(8,128)(2,1)S(1)} %all-to-all-done) | data formatting | bytes 2359296 | tf_op jit(solution)/shard_map/all_to_all | solution.py:50
  74.2 0.0 copy-start.1
  74.2 19.7 %copy.28 = bf16[16,32,12,2,3,16]{5,2,4,3,1,0:T(8,128)(2,1)} copy(bf16[16,32,12,2,3,16]{1,5,4,3,2,0:T(8,128)(2,1)} %bitcast.57) | data formatting | bytes 2359296 | tf_op jit(solution)/shard_map/reshape | solution.py:27
  93.9 0.0 copy-done.1
  93.9 6.6 %convolution_bitcast_fusion = f32[3,16,32,2,16]{4,0,3,2,1:T(4,128)} fusion(bf16[16,32,12,2,3,16]{5,2,4,3,1,0:T(8,128)(2,1)} %copy.28, bf16[16,32,3,12,3,1]{3,2,4,5,1,0:T(4,128)(2,1)S(1)} %copy-done.1), kind=kOutput, calls=%fused_computation.10 | convolution fusion | flops 3538944 | bytes 1486848 | tf_op jit(solution)/shard_map/scepk,scpikh->escih/dot_general | solution.py:28
  100.5 1.8 %copy.30 = f32[3,16,32,2,16]{2,1,0,4,3:T(8,128)S(1)} copy(f32[3,16,32,2,16]{4,0,3,2,1:T(4,128)} %convolution_bitcast_fusion) | data formatting | bytes 393216 | tf_op jit(solution)/shard_map/scepk,scpikh->escih/transpose | solution.py:28
  102.4 0.3 reshape.104
  102.7 2.2 %fusion.2 = f32[32,384]{0,1:T(8,128)S(1)} fusion(f32[1536,32]{0,1:T(8,128)S(1)} %reshape.104, s32[1536]{0:T(1024)S(1)} %eq.15), kind=kOutput, calls=%fused_computation.8 | convolution fusion | flops 227082240 | bytes 251904 | tf_op jit(solution)/shard_map/ra,re->ae/dot_general | solution.py:57
  104.9 0.6 gather_fusion.1
  105.5 5.4 %collective-permute-start = (f32[32,32]{0,1:T(8,128)S(1)}, f32[32,32]{0,1:T(8,128)S(1)}, u32[]{:S(2)}, u32[]{:S(2)}) collective-permute-start(f32[32,32]{0,1:T(8,128)S(1)} %bitcast.61), channel_id=1, source_target_pairs={{0,2},{2,4},{4,6},{6,8},{8,10},{10,12},{12,14},{14,16},{16,18},{18... | collective-permute-start | bytes 12296 | tf_op jit(solution)/shard_map/ppermute | solution.py:18
  111.0 0.6 gather_fusion.2
  111.5 1.9 %collective-permute-start.1 = (f32[32,32]{0,1:T(8,128)S(1)}, f32[32,32]{0,1:T(8,128)S(1)}, u32[]{:S(2)}, u32[]{:S(2)}) collective-permute-start(f32[32,32]{0,1:T(8,128)S(1)} %bitcast.60), channel_id=1, source_target_pairs={{2,0},{4,2},{6,4},{8,6},{10,8},{12,10},{14,12},{16,14},{18,16},{20... | collective-permute-start | bytes 12296 | tf_op jit(solution)/shard_map/ppermute | solution.py:19
  113.5 0.0 collective-permute-done
  113.5 0.8 scatter_custom_fusion
  114.3 4.6 %collective-permute-done.1 = f32[32,32]{0,1:T(8,128)S(1)} collective-permute-done((f32[32,32]{0,1:T(8,128)S(1)}, f32[32,32]{0,1:T(8,128)S(1)}, u32[]{:S(2)}, u32[]{:S(2)}) %collective-permute-start.1) | collective-permute-done | bytes 4128 | tf_op jit(solution)/shard_map/ppermute | solution.py:19
  119.0 0.8 scatter_custom_fusion.1
  119.8 0.7 copy.34
  (4 shorter events, 0.1 us)
Async XLA Ops:
  0.0 1.5 %copy-start = (bf16[8,2,3,32,256]{4,3,2,1,0:T(8,128)(2,1)S(1)}, bf16[8,2,3,32,256]{4,3,2,1,0:T(8,128)(2,1)}, u32[]{:S(2)}) copy-start(bf16[8,2,3,32,256]{4,3,2,1,0:T(8,128)(2,1)} %param.6) | copy-start | bytes 2359300
  35.4 8.6 %copy-start.2 = (bf16[1,16,32,108]{3,2,1,0:T(8,128)(2,1)S(1)}, bf16[1,16,32,108]{3,2,1,0:T(8,128)(2,1)}, u32[]{:S(2)}) copy-start(bf16[1,16,32,108]{3,2,1,0:T(8,128)(2,1)} %param.9) | copy-start | bytes 331780
  36.6 10.3 %copy-start.3 = (s32[3,1,16,32]{3,2,1,0:T(8,128)S(1)}, s32[3,1,16,32]{3,2,1,0:T(8,128)}, u32[]{:S(2)}) copy-start(s32[3,1,16,32]{3,2,1,0:T(8,128)} %param.10) | copy-start | bytes 18436
  36.6 10.4 %copy-start.4 = (s32[1,2,32]{2,1,0:T(2,128)S(1)}, s32[1,2,32]{2,1,0:T(2,128)}, u32[]{:S(2)}) copy-start(s32[1,2,32]{2,1,0:T(2,128)} %param.11) | copy-start | bytes 772
  36.6 34.2 %all-to-all-start = ((bf16[16,32,1152]{2,1,0:T(8,128)(2,1)}), bf16[16,32,1152]{2,1,0:T(8,128)(2,1)S(1)}, u32[]{:S(2)}, u32[]{:S(2)}) async-start(bf16[16,32,1152]{2,1,0:T(8,128)(2,1)} %broadcast_select_fusion), calls=%async_computation | async-start | bytes 2359296 | tf_op jit(solution)/shard_map/all_to_all | solution.py:50
  74.2 19.7 %copy-start.1 = (bf16[16,32,3,12,3,1]{3,2,4,5,1,0:T(4,128)(2,1)S(1)}, bf16[16,32,3,12,3,1]{3,2,4,5,1,0:T(4,128)(2,1)}, u32[]{:S(2)}) copy-start(bf16[16,32,3,12,3,1]{3,2,4,5,1,0:T(4,128)(2,1)} %copy.37) | copy-start | bytes 331780
  105.5 7.9 %collective-permute-start = (f32[32,32]{0,1:T(8,128)S(1)}, f32[32,32]{0,1:T(8,128)S(1)}, u32[]{:S(2)}, u32[]{:S(2)}) collective-permute-start(f32[32,32]{0,1:T(8,128)S(1)} %bitcast.61), channel_id=1, source_target_pairs={{0,2},{2,4},{4,6},{6,8},{8,10},{10,12},{12,14},{14,16},{16,18},{18... | collective-permute-start | bytes 12296 | tf_op jit(solution)/shard_map/ppermute | solution.py:18
  111.5 7.4 %collective-permute-start.1 = (f32[32,32]{0,1:T(8,128)S(1)}, f32[32,32]{0,1:T(8,128)S(1)}, u32[]{:S(2)}, u32[]{:S(2)}) collective-permute-start(f32[32,32]{0,1:T(8,128)S(1)} %bitcast.60), channel_id=1, source_target_pairs={{2,0},{4,2},{6,4},{8,6},{10,8},{12,10},{14,12},{16,14},{18,16},{20... | collective-permute-start | bytes 12296 | tf_op jit(solution)/shard_map/ppermute | solution.py:19
where the time goes:
time: 121 us
  local copies, waits for them, and re-layouts  48.4 us (40%)
  waiting for transfers between devices  28.4 us (23%)
  starting transfers between devices  14.7 us (12%)
  matrix products  14.2 us (12%)
  blocking collectives  10.3 us (9%)
  other arithmetic  4.39 us (4%)
    all_to_all x1, waiting for transfers between devices, body(): lax.all_to_all(outgoing, 'leaf', split_axis=0, concat_axis=0, tiled=True)  23.8 us
    reshape x1, local copies, waits for them, and re-layouts, tested_slots(): field_view = fields.reshape(peer_count, capacity, QUAD, 2, 3, rhs_count)  19.7 us
    psum x1, blocking collectives, body(): summed = lax.psum(partial_field, 'cone')  10.3 us
    reshape x1, local copies, waits for them, and re-layouts, body(): tri_rows = rhs_share.reshape(leaf_count * TRI_LEAF, -1)  9.31 us
    all_to_all x1, starting transfers between devices, body(): lax.all_to_all(outgoing, 'leaf', split_axis=0, concat_axis=0, tiled=True)  7.4 us
    convert_element_type x2, local copies, waits for them, and re-layouts, body(): rhs_share = rhs_share.astype(jnp.bfloat16)  6.78 us
    dot_general x1, matrix products, tested_slots(): jnp.einsum('scepk,scpikh->' + result_form, weight_view, field_view, prefe...  6.63 us
    ppermute x1, starting transfers between devices, extended(): before = lax.ppermute(last, axis, up)  5.42 us
  transfers between devices with their start and end apart: 3, of which 2 were waited for; matrix products, arithmetic and copies ran while one was open for 4% of the time, Pallas kernels for 0%

commit v1 on v0

--- a/solution.py
+++ b/solution.py
@@ -6,6 +6,18 @@
 QUAD = 12
 TRI_LEAF = 32
 EDGE_DEV = 384
+
+
+def split_up(shard, dim, length):
+    shape = shard.shape
+    parts = shard.reshape(*shape[:dim], length, shape[dim] // length, *shape[dim + 1 :])
+    return jnp.moveaxis(parts, dim, 0)
+
+
+def joined_along(parts, dim):
+    shape = list(parts.shape[1:])
+    shape[dim] *= parts.shape[0]
+    return jnp.moveaxis(parts, 0, dim).reshape(shape)
 
 
 def extended(array, sides, width):
@@ -47,7 +59,14 @@
     picked = tri_rows[safe_rows]
     outgoing = jnp.where(is_live[:, :, None], picked, jnp.zeros((), jnp.bfloat16))
     weights = test_weight[0]
-    arrived = lax.all_to_all(outgoing, "leaf", split_axis=0, concat_axis=0, tiled=True)
+    peers_2, here = (lax.axis_size("leaf"), lax.axis_index("leaf"))
+    parts = split_up(outgoing, 0, peers_2)
+    done = [parts[here]]
+    for step in range(1, peers_2):
+        sent = parts[here ^ step]
+        done.append(lax.ppermute(sent, "leaf", [(i_2, i_2 ^ step) for i_2 in range(peers_2)]))
+    parts = jnp.stack(done)[here ^ jnp.arange(peers_2)]
+    arrived = joined_along(parts, 0)
     partial_value = tested_slots(weights, arrived, rhs_count, "escih")
     edge_ids = slot_edge[:, 0].reshape(-1)
     values = partial_value.reshape(-1, 2 * rhs_count)

time: 121 us -> 133 us (1.099)
  waiting for transfers between devices: 28.4 us -> 7.32 us
  starting transfers between devices: 14.7 us -> 33.5 us
  local copies, waits for them, and re-layouts: 48.4 us -> 62.9 us
    ppermute x0 -> x15, starting transfers between devices: none -> 26.5 us  [body(): lax.ppermute(sent, 'leaf', [(i_2, i_2 ^ step) for i_2 in range(peers_2)])]
    all_to_all x1 -> x0, waiting for transfers between devices: 23.8 us -> none  [body(): lax.all_to_all(outgoing, 'leaf', split_axis=0, concat_axis=0, tiled=True)]
    another operation x0 -> x2, local copies, waits for them, and re-layouts: none -> 20.1 us  [the longest x1 19.5 us: tested_slots(): field_view = fields.reshape(peer_count, capacity, QUAD, 2, 3, rhs_count)]
    reshape x1 -> x0, local copies, waits for them, and re-layouts: 19.7 us -> none  [tested_slots(): field_view = fields.reshape(peer_count, capacity, QUAD, 2, 3, rhs_count)]
    unnamed x11 -> x32, local copies, waits for them, and re-layouts: 0.41 us -> 12.4 us
    all_to_all x1 -> x0, starting transfers between devices: 7.4 us -> none  [body(): lax.all_to_all(outgoing, 'leaf', split_axis=0, concat_axis=0, tiled=True)]
    gather x0 -> x2, local copies, waits for them, and re-layouts: none -> 5.34 us  [body(): parts = jnp.stack(done)[here ^ jnp.arange(peers_2)]]
    all_to_all x1 -> x0, local copies, waits for them, and re-layouts: 3.34 us -> none  [body(): lax.all_to_all(outgoing, 'leaf', split_axis=0, concat_axis=0, tiled=True)]
  transfers between devices with their start and end apart: 3 -> 17, of which waited for: 2 -> 2; matrix products, arithmetic and copies ran while one was open for 4% -> 11% of each run, Pallas kernels for 0% -> 0%
where the time goes in v1:
time: 133 us
  local copies, waits for them, and re-layouts  62.9 us (47%)
  starting transfers between devices  33.5 us (25%)
  matrix products  14.2 us (11%)
  blocking collectives  10.3 us (8%)
  waiting for transfers between devices  7.32 us (6%)
  other arithmetic  4.21 us (3%)
    ppermute x15, starting transfers between devices, body(): lax.ppermute(sent, 'leaf', [(i_2, i_2 ^ step) for i_2 in range(peers_2)])  26.5 us
    another operation x1, local copies, waits for them, and re-layouts, tested_slots(): field_view = fields.reshape(peer_count, capacity, QUAD, 2, 3, rhs_count)  19.5 us
    unnamed x32, local copies, waits for them, and re-layouts  12.4 us
    psum x1, blocking collectives, body(): summed = lax.psum(partial_field, 'cone')  10.3 us
    reshape x1, local copies, waits for them, and re-layouts, body(): tri_rows = rhs_share.reshape(leaf_count * TRI_LEAF, -1)  9.31 us
    convert_element_type x2, local copies, waits for them, and re-layouts, body(): rhs_share = rhs_share.astype(jnp.bfloat16)  6.76 us
    dot_general x1, matrix products, tested_slots(): jnp.einsum('scepk,scpikh->' + result_form, weight_view, field_view, prefe...  6.61 us
    gather x2, local copies, waits for them, and re-layouts, body(): parts = jnp.stack(done)[here ^ jnp.arange(peers_2)]  5.34 us
  transfers between devices with their start and end apart: 17, of which 2 were waited for; matrix products, arithmetic and copies ran while one was open for 11% of the time, Pallas kernels for 0%

profile of v1, /device:TPU:6, one launch (start us, length us, event | category | flops | bytes accessed | tf_op | source)
XLA Modules:
  0.0 132.7 jit_solution(3178544981450626007)
XLA Ops:
  0.0 0.8 compare_select_fusion
  0.8 0.7 compare_bitcast_fusion
  1.5 5.3 %fusion.3 = f32[8,768,3,32]{1,3,2,0:T(8,128)} fusion(bf16[8,2,3,32,256]{4,3,2,1,0:T(8,128)(2,1)S(1)} %copy-done, bf16[8,2,256,768]{3,2,1,0:T(8,128)(2,1)} %param.7), kind=kOutput, calls=%fused_computation.10 | convolution fusion | flops 603979776 | bytes 9437184 | tf_op jit(solution)/shard_map/lkchr,lkrq->lqch/dot_general | solution.py:46
  6.8 10.3 %all-reduce.1 = bf16[8,768,3,32]{1,3,2,0:T(8,128)(2,1)S(1)} all-reduce(f32[8,768,3,32]{1,3,2,0:T(8,128)} %fusion.3), channel_id=1, replica_groups=mesh['leaf'=16,'cone'=2] {'cone'}, use_global_device_ids=true, to_apply=%region_0.0 | all-reduce | flops 589824 | bytes 3538944 | tf_op jit(solution)/shard_map/psum | solution.py:51
  17.1 6.7 %copy.24 = bf16[8,768,3,16]{3,2,1,0:T(4,128)(2,1)} copy(bf16[8,768,3,16]{1,3,2,0:T(8,128)(2,1)S(1)} %dynamic-slice_convert_fusion) | data formatting | bytes 1179648 | tf_op jit(solution)/shard_map/convert_element_type | solution.py:53
  23.9 9.3 %reshape.147 = bf16[256,1152]{1,0:T(8,128)(2,1)S(1)} reshape(bf16[8,768,3,16]{3,2,1,0:T(4,128)(2,1)} %copy.24) | data formatting | bytes 1179648 | tf_op jit(solution)/shard_map/reshape | solution.py:55
  33.2 0.1 reshape.152
  33.3 2.1 %gather_fusion = bf16[512,1152]{1,0:T(8,128)(2,1)S(1)} fusion(bf16[256,1152]{1,0:T(8,128)(2,1)S(1)} %reshape.147, s32[1024]{0:T(1024)S(1)} %pad_clamp_fusion.3), kind=kCustom, calls=%fused_computation | custom fusion | bytes 2361344 | tf_op jit(solution)/shard_map/gather | solution.py:59
  35.5 0.2 broadcast_select_fusion
  35.7 1.0 copy-done.1
  36.7 0.9 constant_dynamic-slice_fusion
  37.6 0.6 collective-permute-start
  38.2 0.0 collective-permute-start.1
  38.2 2.9 %collective-permute-start.2 = (bf16[1,32,1152]{2,1,0:T(8,128)(2,1)}, bf16[1,32,1152]{2,1,0:T(8,128)(2,1)S(1)}, u32[]{:S(2)}, u32[]{:S(2)}) collective-permute-start(bf16[1,32,1152]{2,1,0:T(8,128)(2,1)} %get-tuple-element.17), channel_id=1, source_target_pairs={{0,6},{2,4},{4,2},{6,0},{8,14},{10,12},{12,10},{14,8},{16,22},{18,... | collective-permute-start | bytes 221192 | tf_op jit(solution)/shard_map/ppermute | solution.py:67
  41.2 1.6 %collective-permute-start.3 = (bf16[1,32,1152]{2,1,0:T(8,128)(2,1)}, bf16[1,32,1152]{2,1,0:T(8,128)(2,1)S(1)}, u32[]{:S(2)}, u32[]{:S(2)}) collective-permute-start(bf16[1,32,1152]{2,1,0:T(8,128)(2,1)} %get-tuple-element.16), channel_id=1, source_target_pairs={{0,8},{2,10},{4,12},{6,14},{8,0},{10,2},{12,4},{14,6},{16,24},{18,... | collective-permute-start | bytes 221192 | tf_op jit(solution)/shard_map/ppermute | solution.py:67
  42.7 0.4 collective-permute-start.4
  43.2 1.5 %bitcast_dynamic-update-slice_fusion.15 = bf16[16,1,32,1152]{3,2,0,1:T(8,128)(2,1)} fusion(bf16[16,32,1152]{2,1,0:T(8,128)(2,1)} %copy-done.1, s32[]{:T(128)S(6)} %select_n.112), kind=kLoop, calls=%fused_computation.30 | loop fusion | bytes 147460
  44.7 0.4 copy.40
  45.1 1.6 %copy.50 = bf16[16,32,3,12,3,1]{3,2,4,5,1,0:T(4,128)(2,1)S(1)} copy(bf16[16,32,3,12,3,1]{1,0,4,3,2,5:T(8,128)(2,1)S(1)} %bitcast.122) | data formatting | bytes 221184 | tf_op jit(solution)/shard_map/reshape;squeeze | solution.py:38
  46.7 0.1 eq.15
  46.8 0.5 copy-done.5
  47.4 0.6 pad_clamp_fusion
  48.0 0.0 collective-permute-done
  48.0 1.6 %collective-permute-start.5 = (bf16[1,32,1152]{2,1,0:T(8,128)(2,1)S(1)}, bf16[1,32,1152]{2,1,0:T(8,128)(2,1)S(1)}, u32[]{:S(2)}, u32[]{:S(2)}) collective-permute-start(bf16[1,32,1152]{2,1,0:T(8,128)(2,1)S(1)} %get-tuple-element.14), channel_id=1, source_target_pairs={{0,12},{2,14},{4,8},{6,10},{8,4},{10,6},{12,0},{14,2},{16,28},{18,... | collective-permute-start | bytes 221192 | tf_op jit(solution)/shard_map/ppermute | solution.py:67
  49.5 0.6 bitcast_dynamic-update-slice_fusion.13
  50.2 2.3 %collective-permute-start.6 = (bf16[1,32,1152]{2,1,0:T(8,128)(2,1)}, bf16[1,32,1152]{2,1,0:T(8,128)(2,1)S(1)}, u32[]{:S(2)}, u32[]{:S(2)}) collective-permute-start(bf16[1,32,1152]{2,1,0:T(8,128)(2,1)} %get-tuple-element.13), channel_id=1, source_target_pairs={{0,14},{2,12},{4,10},{6,8},{8,6},{10,4},{12,2},{14,0},{16,30},{18,... | collective-permute-start | bytes 221192 | tf_op jit(solution)/shard_map/ppermute | solution.py:67
  52.5 0.6 bitcast_dynamic-update-slice_fusion.12
  53.2 2.6 %collective-permute-start.7 = (bf16[1,32,1152]{2,1,0:T(8,128)(2,1)}, bf16[1,32,1152]{2,1,0:T(8,128)(2,1)S(1)}, u32[]{:S(2)}, u32[]{:S(2)}) collective-permute-start(bf16[1,32,1152]{2,1,0:T(8,128)(2,1)} %get-tuple-element.12), channel_id=1, source_target_pairs={{0,16},{2,18},{4,20},{6,22},{8,24},{10,26},{12,28},{14,30},{16,0},... | collective-permute-start | bytes 221192 | tf_op jit(solution)/shard_map/ppermute | solution.py:67
  55.7 0.6 bitcast_dynamic-update-slice_fusion.11
  56.4 0.3 collective-permute-start.8
  56.7 0.6 bitcast_dynamic-update-slice_fusion.10
  57.3 2.5 %collective-permute-start.9 = (bf16[1,32,1152]{2,1,0:T(8,128)(2,1)}, bf16[1,32,1152]{2,1,0:T(8,128)(2,1)S(1)}, u32[]{:S(2)}, u32[]{:S(2)}) collective-permute-start(bf16[1,32,1152]{2,1,0:T(8,128)(2,1)} %get-tuple-element.10), channel_id=1, source_target_pairs={{0,20},{2,22},{4,16},{6,18},{8,28},{10,30},{12,24},{14,26},{16,4},... | collective-permute-start | bytes 221192 | tf_op jit(solution)/shard_map/ppermute | solution.py:67
  59.9 0.6 bitcast_dynamic-update-slice_fusion.9
  60.5 2.2 %collective-permute-start.10 = (bf16[1,32,1152]{2,1,0:T(8,128)(2,1)}, bf16[1,32,1152]{2,1,0:T(8,128)(2,1)S(1)}, u32[]{:S(2)}, u32[]{:S(2)}) collective-permute-start(bf16[1,32,1152]{2,1,0:T(8,128)(2,1)} %get-tuple-element.9), channel_id=1, source_target_pairs={{0,22},{2,20},{4,18},{6,16},{8,30},{10,28},{12,26},{14,24},{16,6},... | collective-permute-start | bytes 221192 | tf_op jit(solution)/shard_map/ppermute | solution.py:67
  62.7 0.6 bitcast_dynamic-update-slice_fusion.8
  63.4 3.6 %collective-permute-start.11 = (bf16[1,32,1152]{2,1,0:T(8,128)(2,1)}, bf16[1,32,1152]{2,1,0:T(8,128)(2,1)S(1)}, u32[]{:S(2)}, u32[]{:S(2)}) collective-permute-start(bf16[1,32,1152]{2,1,0:T(8,128)(2,1)} %get-tuple-element.8), channel_id=1, source_target_pairs={{0,24},{2,26},{4,28},{6,30},{8,16},{10,18},{12,20},{14,22},{16,8},... | collective-permute-start | bytes 221192 | tf_op jit(solution)/shard_map/ppermute | solution.py:67
  67.0 0.6 bitcast_dynamic-update-slice_fusion.7
  67.6 0.2 collective-permute-start.12
  67.8 0.6 bitcast_dynamic-update-slice_fusion.6
  68.4 3.5 %collective-permute-start.13 = (bf16[1,32,1152]{2,1,0:T(8,128)(2,1)S(1)}, bf16[1,32,1152]{2,1,0:T(8,128)(2,1)S(1)}, u32[]{:S(2)}, u32[]{:S(2)}) collective-permute-start(bf16[1,32,1152]{2,1,0:T(8,128)(2,1)S(1)} %copy-done.3), channel_id=1, source_target_pairs={{0,28},{2,30},{4,24},{6,26},{8,20},{10,22},{12,16},{14,18},{16,12}... | collective-permute-start | bytes 221192 | tf_op jit(solution)/shard_map/ppermute | solution.py:67
  72.0 0.6 bitcast_dynamic-update-slice_fusion.5
  72.6 2.1 %collective-permute-start.14 = (bf16[1,32,1152]{2,1,0:T(8,128)(2,1)S(1)}, bf16[1,32,1152]{2,1,0:T(8,128)(2,1)S(1)}, u32[]{:S(2)}, u32[]{:S(2)}) collective-permute-start(bf16[1,32,1152]{2,1,0:T(8,128)(2,1)S(1)} %get-tuple-element.5), channel_id=1, source_target_pairs={{0,30},{2,28},{4,26},{6,24},{8,22},{10,20},{12,18},{14,16},{16,14}... | collective-permute-start | bytes 221192 | tf_op jit(solution)/shard_map/ppermute | solution.py:67
  74.7 0.6 bitcast_dynamic-update-slice_fusion.4
  75.4 0.6 bitcast_dynamic-update-slice_fusion.3
  76.0 0.6 bitcast_dynamic-update-slice_fusion.2
  76.6 0.6 bitcast_dynamic-update-slice_fusion.1
  77.3 0.6 bitcast_dynamic-update-slice_fusion
  77.9 2.8 %collective-permute-done.14 = bf16[1,32,1152]{2,1,0:T(8,128)(2,1)S(1)} collective-permute-done((bf16[1,32,1152]{2,1,0:T(8,128)(2,1)S(1)}, bf16[1,32,1152]{2,1,0:T(8,128)(2,1)S(1)}, u32[]{:S(2)}, u32[]{:S(2)}) %collective-permute-start.14) | collective-permute-done | bytes 73760 | tf_op jit(solution)/shard_map/ppermute | solution.py:67
  80.7 0.6 bitcast_dynamic-update-slice_fusion.14
  81.3 2.0 %gather_fusion.1 = bf16[16,32,1152]{2,1,0:T(8,128)(2,1)S(1)} fusion(bf16[16,32,1152]{2,1,0:T(8,128)(2,1)} %bitcast.123, s32[1024]{0:T(1024)S(1)} %pad_clamp_fusion.2), kind=kCustom, calls=%fused_computation.1 | custom fusion | bytes 2359360 | tf_op jit(solution)/shard_map/gather | solution.py:68
  83.3 3.3 %copy.39 = bf16[16,32,1152]{1,2,0:T(8,128)(2,1)} copy(bf16[16,32,1152]{2,1,0:T(8,128)(2,1)S(1)} %gather_fusion.1) | data formatting | bytes 2359296 | tf_op jit(solution)/shard_map/gather | solution.py:68
  86.7 19.5 %copy.41 = bf16[16,32,12,2,3,16]{5,2,4,3,1,0:T(8,128)(2,1)} copy(bf16[16,32,12,2,3,16]{1,5,4,3,2,0:T(8,128)(2,1)} %bitcast.120) | data formatting | bytes 2359296 | tf_op jit(solution)/shard_map/reshape;reshape | solution.py:39
  106.2 6.6 %convolution_bitcast_fusion = f32[3,16,32,2,16]{4,0,3,2,1:T(4,128)} fusion(bf16[16,32,12,2,3,16]{5,2,4,3,1,0:T(8,128)(2,1)} %copy.41, bf16[16,32,3,12,3,1]{3,2,4,5,1,0:T(4,128)(2,1)S(1)} %copy.50), kind=kOutput, calls=%fused_computation.11 | convolution fusion | flops 3538944 | bytes 1486848 | tf_op jit(solution)/shard_map/scepk,scpikh->escih/dot_general | solution.py:40
  112.8 1.8 %copy.43 = f32[3,16,32,2,16]{2,1,0,4,3:T(8,128)S(1)} copy(f32[3,16,32,2,16]{4,0,3,2,1:T(4,128)} %convolution_bitcast_fusion) | data formatting | bytes 393216 | tf_op jit(solution)/shard_map/scepk,scpikh->escih/transpose | solution.py:40
  114.6 0.3 reshape.148
  114.9 2.2 %fusion.2 = f32[32,384]{0,1:T(8,128)S(1)} fusion(f32[1536,32]{0,1:T(8,128)S(1)} %reshape.148, s32[1536]{0:T(1024)S(1)} %eq.15), kind=kOutput, calls=%fused_computation.9 | convolution fusion | flops 227082240 | bytes 251904 | tf_op jit(solution)/shard_map/ra,re->ae/dot_general | solution.py:76
  117.2 0.7 gather_fusion.2
  117.9 5.1 %collective-permute-start.15 = (f32[32,32]{0,1:T(8,128)S(1)}, f32[32,32]{0,1:T(8,128)S(1)}, u32[]{:S(2)}, u32[]{:S(2)}) collective-permute-start(f32[32,32]{0,1:T(8,128)S(1)} %bitcast.125), channel_id=1, source_target_pairs={{0,2},{2,4},{4,6},{6,8},{8,10},{10,12},{12,14},{14,16},{16,18},{18... | collective-permute-start | bytes 12296 | tf_op jit(solution)/shard_map/ppermute | solution.py:30
  123.0 0.6 gather_fusion.3
  123.6 1.9 %collective-permute-start.16 = (f32[32,32]{0,1:T(8,128)S(1)}, f32[32,32]{0,1:T(8,128)S(1)}, u32[]{:S(2)}, u32[]{:S(2)}) collective-permute-start(f32[32,32]{0,1:T(8,128)S(1)} %bitcast.124), channel_id=1, source_target_pairs={{2,0},{4,2},{6,4},{8,6},{10,8},{12,10},{14,12},{16,14},{18,16},{20... | collective-permute-start | bytes 12296 | tf_op jit(solution)/shard_map/ppermute | solution.py:31
  125.5 1.0 scatter_custom_fusion
  126.5 4.5 %collective-permute-done.16 = f32[32,32]{0,1:T(8,128)S(1)} collective-permute-done((f32[32,32]{0,1:T(8,128)S(1)}, f32[32,32]{0,1:T(8,128)S(1)}, u32[]{:S(2)}, u32[]{:S(2)}) %collective-permute-start.16) | collective-permute-done | bytes 4128 | tf_op jit(solution)/shard_map/ppermute | solution.py:31
  131.0 0.9 scatter_custom_fusion.1
  132.0 0.7 copy.47
  (33 shorter events, 0.1 us)
Async XLA Ops:
  0.0 1.5 %copy-start = (bf16[8,2,3,32,256]{4,3,2,1,0:T(8,128)(2,1)S(1)}, bf16[8,2,3,32,256]{4,3,2,1,0:T(8,128)(2,1)}, u32[]{:S(2)}) copy-start(bf16[8,2,3,32,256]{4,3,2,1,0:T(8,128)(2,1)} %param.6) | copy-start | bytes 2359300
  35.7 1.1 copy-start.1
  36.7 7.9 %copy-start.2 = (bf16[1,16,32,108]{3,2,1,0:T(8,128)(2,1)S(1)}, bf16[1,16,32,108]{3,2,1,0:T(8,128)(2,1)}, u32[]{:S(2)}) copy-start(bf16[1,16,32,108]{3,2,1,0:T(8,128)(2,1)} %param.9) | copy-start | bytes 331780
  37.6 10.3 %collective-permute-start = (bf16[1,32,1152]{2,1,0:T(8,128)(2,1)S(1)}, bf16[1,32,1152]{2,1,0:T(8,128)(2,1)S(1)}, u32[]{:S(2)}, u32[]{:S(2)}) collective-permute-start(bf16[1,32,1152]{2,1,0:T(8,128)(2,1)S(1)} %get-tuple-element.19), channel_id=1, source_target_pairs={{0,2},{2,0},{4,6},{6,4},{8,10},{10,8},{12,14},{14,12},{16,18},{18,... | collective-permute-start | bytes 221192 | tf_op jit(solution)/shard_map/ppermute | solution.py:67
  38.2 12.0 %collective-permute-start.1 = (bf16[1,32,1152]{2,1,0:T(8,128)(2,1)}, bf16[1,32,1152]{2,1,0:T(8,128)(2,1)S(1)}, u32[]{:S(2)}, u32[]{:S(2)}) collective-permute-start(bf16[1,32,1152]{2,1,0:T(8,128)(2,1)} %get-tuple-element.18), channel_id=1, source_target_pairs={{0,4},{2,6},{4,0},{6,2},{8,12},{10,14},{12,8},{14,10},{16,20},{18,... | collective-permute-start | bytes 221192 | tf_op jit(solution)/shard_map/ppermute | solution.py:67
  38.2 14.9 %collective-permute-start.2 = (bf16[1,32,1152]{2,1,0:T(8,128)(2,1)}, bf16[1,32,1152]{2,1,0:T(8,128)(2,1)S(1)}, u32[]{:S(2)}, u32[]{:S(2)}) collective-permute-start(bf16[1,32,1152]{2,1,0:T(8,128)(2,1)} %get-tuple-element.17), channel_id=1, source_target_pairs={{0,6},{2,4},{4,2},{6,0},{8,14},{10,12},{12,10},{14,8},{16,22},{18,... | collective-permute-start | bytes 221192 | tf_op jit(solution)/shard_map/ppermute | solution.py:67
  41.2 15.2 %collective-permute-start.3 = (bf16[1,32,1152]{2,1,0:T(8,128)(2,1)}, bf16[1,32,1152]{2,1,0:T(8,128)(2,1)S(1)}, u32[]{:S(2)}, u32[]{:S(2)}) collective-permute-start(bf16[1,32,1152]{2,1,0:T(8,128)(2,1)} %get-tuple-element.16), channel_id=1, source_target_pairs={{0,8},{2,10},{4,12},{6,14},{8,0},{10,2},{12,4},{14,6},{16,24},{18,... | collective-permute-start | bytes 221192 | tf_op jit(solution)/shard_map/ppermute | solution.py:67
  42.7 14.6 %collective-permute-start.4 = (bf16[1,32,1152]{2,1,0:T(8,128)(2,1)}, bf16[1,32,1152]{2,1,0:T(8,128)(2,1)S(1)}, u32[]{:S(2)}, u32[]{:S(2)}) collective-permute-start(bf16[1,32,1152]{2,1,0:T(8,128)(2,1)} %get-tuple-element.15), channel_id=1, source_target_pairs={{0,10},{2,8},{4,14},{6,12},{8,2},{10,0},{12,6},{14,4},{16,26},{18,... | collective-permute-start | bytes 221192 | tf_op jit(solution)/shard_map/ppermute | solution.py:67
  44.7 2.1 %copy-start.7 = (s32[1,2,32]{2,1,0:T(2,128)S(1)}, s32[1,2,32]{2,1,0:T(2,128)}, u32[]{:S(2)}) copy-start(s32[1,2,32]{2,1,0:T(2,128)} %param.11) | copy-start | bytes 772
  45.1 1.6 %copy-start.4 = (s32[3,1,16,32]{3,2,1,0:T(8,128)S(1)}, s32[3,1,16,32]{3,2,1,0:T(8,128)}, u32[]{:S(2)}) copy-start(s32[3,1,16,32]{3,2,1,0:T(8,128)} %param.10) | copy-start | bytes 18436
  45.1 23.4 %copy-start.3 = (bf16[1,32,1152]{2,1,0:T(8,128)(2,1)S(1)}, bf16[1,32,1152]{2,1,0:T(8,128)(2,1)}, u32[]{:S(2)}) copy-start(bf16[1,32,1152]{2,1,0:T(8,128)(2,1)} %get-tuple-element.6) | copy-start | bytes 221188
  46.8 0.6 copy-start.5
  46.8 34.5 %copy-start.6 = (s32[32]{0:T(128)}, s32[32]{0:T(128)S(1)}, u32[]{:S(2)}) copy-start(s32[32]{0:T(128)S(1)} %get-tuple-element.21) | copy-start | bytes 388
  48.0 12.5 %collective-permute-start.5 = (bf16[1,32,1152]{2,1,0:T(8,128)(2,1)S(1)}, bf16[1,32,1152]{2,1,0:T(8,128)(2,1)S(1)}, u32[]{:S(2)}, u32[]{:S(2)}) collective-permute-start(bf16[1,32,1152]{2,1,0:T(8,128)(2,1)S(1)} %get-tuple-element.14), channel_id=1, source_target_pairs={{0,12},{2,14},{4,8},{6,10},{8,4},{10,6},{12,0},{14,2},{16,28},{18,... | collective-permute-start | bytes 221192 | tf_op jit(solution)/shard_map/ppermute | solution.py:67
  50.2 13.2 %collective-permute-start.6 = (bf16[1,32,1152]{2,1,0:T(8,128)(2,1)}, bf16[1,32,1152]{2,1,0:T(8,128)(2,1)S(1)}, u32[]{:S(2)}, u32[]{:S(2)}) collective-permute-start(bf16[1,32,1152]{2,1,0:T(8,128)(2,1)} %get-tuple-element.13), channel_id=1, source_target_pairs={{0,14},{2,12},{4,10},{6,8},{8,6},{10,4},{12,2},{14,0},{16,30},{18,... | collective-permute-start | bytes 221192 | tf_op jit(solution)/shard_map/ppermute | solution.py:67
  53.2 14.4 %collective-permute-start.7 = (bf16[1,32,1152]{2,1,0:T(8,128)(2,1)}, bf16[1,32,1152]{2,1,0:T(8,128)(2,1)S(1)}, u32[]{:S(2)}, u32[]{:S(2)}) collective-permute-start(bf16[1,32,1152]{2,1,0:T(8,128)(2,1)} %get-tuple-element.12), channel_id=1, source_target_pairs={{0,16},{2,18},{4,20},{6,22},{8,24},{10,26},{12,28},{14,30},{16,0},... | collective-permute-start | bytes 221192 | tf_op jit(solution)/shard_map/ppermute | solution.py:67
  56.4 12.1 %collective-permute-start.8 = (bf16[1,32,1152]{2,1,0:T(8,128)(2,1)}, bf16[1,32,1152]{2,1,0:T(8,128)(2,1)S(1)}, u32[]{:S(2)}, u32[]{:S(2)}) collective-permute-start(bf16[1,32,1152]{2,1,0:T(8,128)(2,1)} %get-tuple-element.11), channel_id=1, source_target_pairs={{0,18},{2,16},{4,22},{6,20},{8,26},{10,24},{12,30},{14,28},{16,2},... | collective-permute-start | bytes 221192 | tf_op jit(solution)/shard_map/ppermute | solution.py:67
  57.3 15.3 %collective-permute-start.9 = (bf16[1,32,1152]{2,1,0:T(8,128)(2,1)}, bf16[1,32,1152]{2,1,0:T(8,128)(2,1)S(1)}, u32[]{:S(2)}, u32[]{:S(2)}) collective-permute-start(bf16[1,32,1152]{2,1,0:T(8,128)(2,1)} %get-tuple-element.10), channel_id=1, source_target_pairs={{0,20},{2,22},{4,16},{6,18},{8,28},{10,30},{12,24},{14,26},{16,4},... | collective-permute-start | bytes 221192 | tf_op jit(solution)/shard_map/ppermute | solution.py:67
  60.5 14.9 %collective-permute-start.10 = (bf16[1,32,1152]{2,1,0:T(8,128)(2,1)}, bf16[1,32,1152]{2,1,0:T(8,128)(2,1)S(1)}, u32[]{:S(2)}, u32[]{:S(2)}) collective-permute-start(bf16[1,32,1152]{2,1,0:T(8,128)(2,1)} %get-tuple-element.9), channel_id=1, source_target_pairs={{0,22},{2,20},{4,18},{6,16},{8,30},{10,28},{12,26},{14,24},{16,6},... | collective-permute-start | bytes 221192 | tf_op jit(solution)/shard_map/ppermute | solution.py:67
  63.4 12.6 %collective-permute-start.11 = (bf16[1,32,1152]{2,1,0:T(8,128)(2,1)}, bf16[1,32,1152]{2,1,0:T(8,128)(2,1)S(1)}, u32[]{:S(2)}, u32[]{:S(2)}) collective-permute-start(bf16[1,32,1152]{2,1,0:T(8,128)(2,1)} %get-tuple-element.8), channel_id=1, source_target_pairs={{0,24},{2,26},{4,28},{6,30},{8,16},{10,18},{12,20},{14,22},{16,8},... | collective-permute-start | bytes 221192 | tf_op jit(solution)/shard_map/ppermute | solution.py:67
  67.6 9.0 %collective-permute-start.12 = (bf16[1,32,1152]{2,1,0:T(8,128)(2,1)}, bf16[1,32,1152]{2,1,0:T(8,128)(2,1)S(1)}, u32[]{:S(2)}, u32[]{:S(2)}) collective-permute-start(bf16[1,32,1152]{2,1,0:T(8,128)(2,1)} %get-tuple-element.7), channel_id=1, source_target_pairs={{0,26},{2,24},{4,30},{6,28},{8,18},{10,16},{12,22},{14,20},{16,10}... | collective-permute-start | bytes 221192 | tf_op jit(solution)/shard_map/ppermute | solution.py:67
  68.4 8.8 %collective-permute-start.13 = (bf16[1,32,1152]{2,1,0:T(8,128)(2,1)S(1)}, bf16[1,32,1152]{2,1,0:T(8,128)(2,1)S(1)}, u32[]{:S(2)}, u32[]{:S(2)}) collective-permute-start(bf16[1,32,1152]{2,1,0:T(8,128)(2,1)S(1)} %copy-done.3), channel_id=1, source_target_pairs={{0,28},{2,30},{4,24},{6,26},{8,20},{10,22},{12,16},{14,18},{16,12}... | collective-permute-start | bytes 221192 | tf_op jit(solution)/shard_map/ppermute | solution.py:67
  72.6 8.1 %collective-permute-start.14 = (bf16[1,32,1152]{2,1,0:T(8,128)(2,1)S(1)}, bf16[1,32,1152]{2,1,0:T(8,128)(2,1)S(1)}, u32[]{:S(2)}, u32[]{:S(2)}) collective-permute-start(bf16[1,32,1152]{2,1,0:T(8,128)(2,1)S(1)} %get-tuple-element.5), channel_id=1, source_target_pairs={{0,30},{2,28},{4,26},{6,24},{8,22},{10,20},{12,18},{14,16},{16,14}... | collective-permute-start | bytes 221192 | tf_op jit(solution)/shard_map/ppermute | solution.py:67
  117.9 7.6 %collective-permute-start.15 = (f32[32,32]{0,1:T(8,128)S(1)}, f32[32,32]{0,1:T(8,128)S(1)}, u32[]{:S(2)}, u32[]{:S(2)}) collective-permute-start(f32[32,32]{0,1:T(8,128)S(1)} %bitcast.125), channel_id=1, source_target_pairs={{0,2},{2,4},{4,6},{6,8},{8,10},{10,12},{12,14},{14,16},{16,18},{18... | collective-permute-start | bytes 12296 | tf_op jit(solution)/shard_map/ppermute | solution.py:30
  123.6 7.4 %collective-permute-start.16 = (f32[32,32]{0,1:T(8,128)S(1)}, f32[32,32]{0,1:T(8,128)S(1)}, u32[]{:S(2)}, u32[]{:S(2)}) collective-permute-start(f32[32,32]{0,1:T(8,128)S(1)} %bitcast.124), channel_id=1, source_target_pairs={{2,0},{4,2},{6,4},{8,6},{10,8},{12,10},{14,12},{16,14},{18,16},{20... | collective-permute-start | bytes 12296 | tf_op jit(solution)/shard_map/ppermute | solution.py:31
